TPU v7x, 32 devices: a whole 2x2x4 slice. The times are simulated.
32 devices in a mesh: blk: 8 (over z, y), team: 4 (over x, core).
Axes of the slice: x: 2, y: 2, z: 4, core: 2. Of those that a mesh axis runs over, the one named last changes fastest.
Arguments:
- omega: float32 [8, 8, 128, 128], P('blk'), may hold values from -0.05 to 2, as said below
- dosage: float32 [8, 256, 128], P('blk', 'team'), may hold values from -6 to 6
- columns: int32 [8, 8], P('blk'), may hold values from 0 to 7, as said below
- counts: int32 [8], P('blk'), may hold values from 1 to 4, as said below
Outputs:
- new_omega: float32 [8, 8, 128, 128], P('blk')
- y_product: float32 [8, 256, 128], P('blk', 'team')
Inputs may be any that keep to these rules, and one draw needn't show every extreme that they name: The first counts[b] slots of row b hold distinct block columns in ascending order, b among them; the pattern is symmetric (c is listed in row b exactly when b is listed in row c); every live column c of row b has |c - b| <= 1, or (c - b) mod 8 equal to f or 8 - f for one of the offsets f = 4 - j * 2, j = 0 to 0, and every row is linked at all these distant offsets; the other slots hold b. `counts`: some block row has exactly 4 in every draw. `omega`: symmetric: the block in row b for column c is the transpose of the block in row c for column b; diagonal entries of diagonal blocks lie in 1 to 2, all other entries in -0.05 to 0.05.
All inputs are finite; a program needn't handle non-finite values.
Results may differ from a plain program's by a relative error of at most 0.0003.
Values sent between devices are 32-bit elements; how exact they have to be, the bound alone decides.
A program may use at most 64 MiB of HBM per device.

v0:
```python
import jax
import jax.numpy as jnp
from jax import lax
from jax.sharding import PartitionSpec as P

step_size = 0.1
penalty = 0.05


def shifted(block, axis, distance):
    devices = range(lax.axis_size(axis))
    route = [((i - distance) % len(devices), i) for i in devices]
    return lax.ppermute(block, axis, route)


def per_device(omega, dosage, columns, counts):
    highest = lax.Precision.HIGHEST
    weights = omega[0]
    own_dosage = dosage[0]
    links = columns[0]
    slot_count = weights.shape[0]
    block_size = weights.shape[1]
    samples_here = own_dosage.shape[0]
    owner = lax.axis_index("blk")
    row_total = lax.axis_size("blk")
    team_size = lax.axis_size("team")
    samples = samples_here * team_size
    live = jnp.arange(slot_count, dtype=jnp.int32) < counts[0]
    reach_near = max(1, row_total // 16)
    far_count = max(1, row_total // 32)
    far_stride = max(1, (row_total // 2 - 1 - reach_near) // far_count)
    distances = []
    for distance in range(1, reach_near + 1):
        distances.append(distance)
        distances.append(-distance)
    for number in range(far_count):
        distance = row_total // 2 - number * far_stride
        distances.append(distance)
        if 2 * distance != row_total:
            distances.append(-distance)

    def arrange(own_block, arrivals):
        placed = jnp.where((live & (links == owner))[:, None, None], own_block[None], 0.0)
        for distance, block in zip(distances, arrivals):
            target = jnp.mod(owner + distance, row_total)
            match = live & (links == target)
            placed = jnp.where(match[:, None, None], block[None], placed)
        return placed

    dosage_arrivals = [shifted(dosage, "blk", -distance)[0] for distance in distances]
    placed_dosage = arrange(own_dosage, dosage_arrivals)
    product = jnp.einsum("ksb,kab->sa", placed_dosage, weights, precision=highest)
    y_product = product[None]
    product_arrivals = [shifted(y_product, "blk", -distance)[0] for distance in distances]
    placed_product = arrange(product, product_arrivals)
    tiles = jnp.einsum("sa,ksb->kab", product, placed_dosage, precision=highest)
    tiles = tiles + jnp.einsum("sa,ksb->kab", own_dosage, placed_product, precision=highest)
    unit = jnp.eye(block_size, dtype=bool)
    on_diag = live & (links == owner)
    diag_values = jnp.sum(
        jnp.where(on_diag[:, None], jnp.diagonal(weights, axis1=1, axis2=2), 0.0), axis=0
    )
    inverse = 1.0 / diag_values
    summed = lax.psum(tiles, "team")
    grad = summed / (2.0 * samples)
    corner = (live & (links == owner))[:, None, None] & unit[None]
    grad = grad - jnp.where(corner, inverse[None, None, :], 0.0)
    moved = weights - step_size * grad
    shrunk = jnp.sign(moved) * jnp.maximum(jnp.abs(moved) - step_size * penalty, 0.0)
    result = jnp.where(corner, moved, shrunk)
    new_omega = jnp.where(live[:, None, None], result, 0.0)
    return (new_omega[None], y_product)


def solution(mesh):
    return jax.shard_map(
        per_device,
        mesh=mesh,
        in_specs=(P("blk", None, None, None), P("blk", "team", None), P("blk", None), P("blk")),
        out_specs=(P("blk", None, None, None), P("blk", "team", None)),
        check_vma=False,
    )
```

profile of v0, /device:TPU:0, one launch (start us, length us, event | category | flops | bytes accessed | tf_op | source)
XLA Modules:
  0.0 79.1 jit_solution(14924596702063830044)
XLA Ops:
  7.2 0.0 copy-start.1
  7.2 0.0 copy-start
  7.2 0.0 copy-start.3
  7.2 0.0 all-reduce.2.cloned.1.call-start
  7.2 4.1 %collective-permute-start = (f32[1,64,128]{2,1,0:T(8,128)}, f32[1,64,128]{2,1,0:T(8,128)S(1)}, u32[]{:S(2)}, u32[]{:S(2)}) collective-permute-start(f32[1,64,128]{2,1,0:T(8,128)} %param.5), channel_id=1, source_target_pairs={{16,0},{20,4},{24,8},{28,12},{0,16},{4,20},{8,24},{12,28},{17,1},{... | collective-permute-start | bytes 98312 | tf_op jit(solution)/shard_map/ppermute | solution.py:13
  11.3 1.5 %collective-permute-start.1 = (f32[1,64,128]{2,1,0:T(8,128)}, f32[1,64,128]{2,1,0:T(8,128)S(1)}, u32[]{:S(2)}, u32[]{:S(2)}) collective-permute-start(f32[1,64,128]{2,1,0:T(8,128)} %param.5), channel_id=1, source_target_pairs={{28,0},{0,4},{4,8},{8,12},{12,16},{16,20},{20,24},{24,28},{29,1},{... | collective-permute-start | bytes 98312 | tf_op jit(solution)/shard_map/ppermute | solution.py:13
  12.9 3.2 %collective-permute-start.2 = (f32[1,64,128]{2,1,0:T(8,128)}, f32[1,64,128]{2,1,0:T(8,128)S(1)}, u32[]{:S(2)}, u32[]{:S(2)}) collective-permute-start(f32[1,64,128]{2,1,0:T(8,128)} %param.5), channel_id=1, source_target_pairs={{4,0},{8,4},{12,8},{16,12},{20,16},{24,20},{28,24},{0,28},{5,1},{9... | collective-permute-start | bytes 98312 | tf_op jit(solution)/shard_map/ppermute | solution.py:13
  16.7 5.9 %copy.8 = f32[8,128,128]{0,2,1:T(8,128)} copy(f32[8,128,128]{2,1,0:T(8,128)} %bitcast.38) | data formatting | bytes 1048576 | tf_op jit(solution)/shard_map/squeeze | solution.py:18
  22.6 1.8 %gather_fusion = f32[128,8]{1,0:T(8,128)S(1)} fusion(f32[8,128,128]{0,2,1:T(8,128)} %copy.8, s32[128]{0:T(128)S(1)} %or_bitcast_fusion), kind=kCustom, calls=%fused_computation | custom fusion | bytes 9216 | tf_op jit(solution)/shard_map/jit(diagonal)/gather | solution.py:61
  24.4 0.0 copy-done.3
  24.4 0.1 select_reduce_fusion
  24.5 0.0 collective-permute-done
  24.5 0.0 collective-permute-done.1
  24.5 0.0 collective-permute-done.2
  24.5 0.0 copy-done.1
  24.5 0.0 copy-done
  24.6 0.7 fusion.11
  25.3 0.0 copy-start.2
  25.3 0.1 collective-permute-start.3
  25.4 0.1 collective-permute-start.4
  25.4 4.7 %collective-permute-start.5 = (f32[1,64,128]{2,1,0:T(8,128)S(1)}, f32[1,64,128]{2,1,0:T(8,128)S(1)}, u32[]{:S(2)}, u32[]{:S(2)}) collective-permute-start(f32[1,64,128]{2,1,0:T(8,128)S(1)} %bitcast.43), channel_id=1, source_target_pairs={{4,0},{8,4},{12,8},{16,12},{20,16},{24,20},{28,24},{0,28},{5,1},{9... | collective-permute-start | bytes 98312 | tf_op jit(solution)/shard_map/ppermute | solution.py:13
  30.2 0.0 collective-permute-done.3
  30.2 1.8 %collective-permute-done.4 = f32[1,64,128]{2,1,0:T(8,128)S(1)} collective-permute-done((f32[1,64,128]{2,1,0:T(8,128)S(1)}, f32[1,64,128]{2,1,0:T(8,128)S(1)}, u32[]{:S(2)}, u32[]{:S(2)}) %collective-permute-start.4) | collective-permute-done | bytes 32800 | tf_op jit(solution)/shard_map/ppermute | solution.py:13
  32.0 0.0 collective-permute-done.5
  32.0 1.1 %fusion.6 = f32[8,128,128]{2,1,0:T(8,128)S(1)} fusion(f32[64,128]{1,0:T(8,128)S(1)} %bitcast.44, f32[64,128]{1,0:T(8,128)S(1)} %bitcast.54, f32[64,128]{1,0:T(8,128)S(1)} %bitcast.53, f32[64,128]{1,0:T(8,128)S(1)} %bitcast.52, pred[8]{0:T(512)(128)(4,1)S(1)} %get-tuple-element.5, pred[8]{0:T(512)(128)(4,1)S(1)} %get-tuple-element.6, ...), kind=kOutput, calls=%fused_computation.10 | convolution fusion | flops 100925440 | bytes 688160 | tf_op jit(solution)/shard_map/sa,ksb->kab/dot_general | solution.py:57
  33.1 1.9 %fusion = f32[8,128,128]{1,2,0:T(8,128)} fusion(f32[8,128,128]{2,1,0:T(8,128)S(1)} %fusion.6, f32[64,128,1]{1,0,2:T(8,128)S(1)} %fusion.11, f32[64,128]{1,0:T(8,128)S(1)} %bitcast.40, f32[64,128]{1,0:T(8,128)S(1)} %bitcast.51, f32[64,128]{1,0:T(8,128)S(1)} %bitcast.49, f32[64,128]{1,0:T(8,128)S(1)} %bitcast.47, pred[8]{0:T(512)(128)(4,1)S(1)} %get-tuple-element.5, ...), kind=kOutput, calls=%fused_computation.2 | convolution fusion | flops 101056512 | bytes 1212448 | tf_op jit(solution)/shard_map/sa,ksb->kab/dot_general | solution.py:56
  35.0 0.0 all-reduce.2.cloned.1.call-update
  35.0 0.2 copy.6
  35.2 34.5 %all-reduce.2.cloned.1.call-done = f32[8,128,128]{1,2,0:T(8,128)} async-done(((f32[8,128,128]{1,2,0:T(8,128)}), f32[8,128,128]{1,2,0:T(8,128)}) %all-reduce.2.cloned.1.call-update) | async-done | bytes 524304 | tf_op jit(solution)/shard_map/psum | solution.py:64
  69.8 1.5 %fusion.5 = f32[1,8,128,128]{2,3,1,0:T(8,128)S(1)} fusion(f32[1,8,128,128]{2,3,1,0:T(8,128)S(1)} %copy.6, f32[8,128,128]{1,2,0:T(8,128)} %all-reduce.2.cloned.1.call-done, f32[128]{0:T(128)S(1)} %broadcast_divide_fusion, pred[8]{0:T(512)(128)(4,1)S(1)} %iota_compare_fusion.1, pred[128,128]{0,1:T(8,128)(4,1)S(1)} %iota_compare_fusion, ...), kind=kLoop, calls=%fused_computation.9 | loop fusion | flops 1703936 | bytes 1589776 | tf_op jit(solution)/shard_map/broadcast_in_dim | solution.py:72
  71.3 1.0 %copy.9 = f32[1,8,128,128]{3,2,1,0:T(8,128)} copy(f32[1,8,128,128]{2,3,1,0:T(8,128)S(1)} %fusion.5) | data formatting | bytes 1048576
  72.3 0.0 copy-done.2
  (5 shorter events, 0.0 us)
Async XLA Ops:
  7.2 17.4 %copy-start.1 = (f32[1,64,128]{2,1,0:T(8,128)S(1)}, f32[1,64,128]{2,1,0:T(8,128)}, u32[]{:S(2)}) copy-start(f32[1,64,128]{2,1,0:T(8,128)} %param.5) | copy-start | bytes 98308
  7.2 17.4 %copy-start = (f32[1,8,128,128]{3,2,1,0:T(8,128)S(1)}, f32[1,8,128,128]{3,2,1,0:T(8,128)}, u32[]{:S(2)}) copy-start(f32[1,8,128,128]{3,2,1,0:T(8,128)} %param.4) | copy-start | bytes 1572868
  7.2 17.2 %copy-start.3 = (s32[1,8]{1,0:T(1,128)S(1)}, s32[1,8]{1,0:T(1,128)}, u32[]{:S(2)}) copy-start(s32[1,8]{1,0:T(1,128)} %param.6) | copy-start | bytes 100
  7.2 62.6 %all-reduce.2.cloned.1.call-start = ((), (), s32[]{:S(2)}) async-start(), calls=%async_computation | async-start | bytes 1048576 | tf_op jit(solution)/shard_map/psum | solution.py:64
  7.2 17.3 %collective-permute-start = (f32[1,64,128]{2,1,0:T(8,128)}, f32[1,64,128]{2,1,0:T(8,128)S(1)}, u32[]{:S(2)}, u32[]{:S(2)}) collective-permute-start(f32[1,64,128]{2,1,0:T(8,128)} %param.5), channel_id=1, source_target_pairs={{16,0},{20,4},{24,8},{28,12},{0,16},{4,20},{8,24},{12,28},{17,1},{... | collective-permute-start | bytes 98312 | tf_op jit(solution)/shard_map/ppermute | solution.py:13
  11.3 13.2 %collective-permute-start.1 = (f32[1,64,128]{2,1,0:T(8,128)}, f32[1,64,128]{2,1,0:T(8,128)S(1)}, u32[]{:S(2)}, u32[]{:S(2)}) collective-permute-start(f32[1,64,128]{2,1,0:T(8,128)} %param.5), channel_id=1, source_target_pairs={{28,0},{0,4},{4,8},{8,12},{12,16},{16,20},{20,24},{24,28},{29,1},{... | collective-permute-start | bytes 98312 | tf_op jit(solution)/shard_map/ppermute | solution.py:13
  12.9 11.7 %collective-permute-start.2 = (f32[1,64,128]{2,1,0:T(8,128)}, f32[1,64,128]{2,1,0:T(8,128)S(1)}, u32[]{:S(2)}, u32[]{:S(2)}) collective-permute-start(f32[1,64,128]{2,1,0:T(8,128)} %param.5), channel_id=1, source_target_pairs={{4,0},{8,4},{12,8},{16,12},{20,16},{24,20},{28,24},{0,28},{5,1},{9... | collective-permute-start | bytes 98312 | tf_op jit(solution)/shard_map/ppermute | solution.py:13
  25.3 47.0 %copy-start.2 = (f32[64,128,1]{1,0,2:T(8,128)}, f32[64,128,1]{1,0,2:T(8,128)S(1)}, u32[]{:S(2)}) copy-start(f32[64,128,1]{1,0,2:T(8,128)S(1)} %fusion.11) | copy-start | bytes 98308
  25.3 4.9 %collective-permute-start.3 = (f32[1,64,128]{2,1,0:T(8,128)S(1)}, f32[1,64,128]{2,1,0:T(8,128)S(1)}, u32[]{:S(2)}, u32[]{:S(2)}) collective-permute-start(f32[1,64,128]{2,1,0:T(8,128)S(1)} %bitcast.41), channel_id=1, source_target_pairs={{16,0},{20,4},{24,8},{28,12},{0,16},{4,20},{8,24},{12,28},{17,1},{... | collective-permute-start | bytes 98312 | tf_op jit(solution)/shard_map/ppermute | solution.py:13
  25.4 6.7 %collective-permute-start.4 = (f32[1,64,128]{2,1,0:T(8,128)S(1)}, f32[1,64,128]{2,1,0:T(8,128)S(1)}, u32[]{:S(2)}, u32[]{:S(2)}) collective-permute-start(f32[1,64,128]{2,1,0:T(8,128)S(1)} %bitcast.42), channel_id=1, source_target_pairs={{28,0},{0,4},{4,8},{8,12},{12,16},{16,20},{20,24},{24,28},{29,1},{... | collective-permute-start | bytes 98312 | tf_op jit(solution)/shard_map/ppermute | solution.py:13
  25.4 6.6 %collective-permute-start.5 = (f32[1,64,128]{2,1,0:T(8,128)S(1)}, f32[1,64,128]{2,1,0:T(8,128)S(1)}, u32[]{:S(2)}, u32[]{:S(2)}) collective-permute-start(f32[1,64,128]{2,1,0:T(8,128)S(1)} %bitcast.43), channel_id=1, source_target_pairs={{4,0},{8,4},{12,8},{16,12},{20,16},{24,20},{28,24},{0,28},{5,1},{9... | collective-permute-start | bytes 98312 | tf_op jit(solution)/shard_map/ppermute | solution.py:13
Sparse Core Ops, SparseCore 0:
  35.1 34.5 all-reduce.1
where the time goes:
time: 79.4 us; the launch traced here: 79.1 us
  waiting for transfers between devices  36.4 us (46%)
  between operations  14.8 us (19%)
  starting transfers between devices  13.7 us (17%)
  local copies, waits for them, and re-layouts  8.85 us (11%)
  matrix products  3.68 us (5%)
  other arithmetic  1.65 us (2%)
    psum x1, waiting for transfers between devices, per_device(): summed = lax.psum(tiles, 'team')  34.5 us
    ppermute x6, starting transfers between devices, shifted(): return lax.ppermute(block, axis, route)  13.7 us
    squeeze x1, local copies, waits for them, and re-layouts, per_device(): weights = omega[0]  5.87 us
    dot_general x1, matrix products, per_device(): tiles = jnp.einsum('sa,ksb->kab', product, placed_dosage, precision=highest)  1.88 us
    ppermute x6, waiting for transfers between devices, shifted(): return lax.ppermute(block, axis, route)  1.88 us
    gather x1, local copies, waits for them, and re-layouts, per_device(): jnp.diagonal(weights, axis1=1, axis2=2)  1.76 us
  transfers between devices with their start and end apart: 7, of which 2 were waited for; matrix products, arithmetic and copies ran while one was open for 10% of the time, Pallas kernels for 0%

commit v1 on v0

v1 whole, which is shorter than its diff:
```python
import jax
import jax.numpy as jnp
from jax import lax
from jax.experimental import pallas as pl
from jax.experimental.pallas import tpu as pltpu
from jax.sharding import PartitionSpec as P

step_size = 0.1
penalty = 0.05
MESH = pl.DeviceIdType.MESH


def link_distances(row_total):
    reach_near = max(1, row_total // 16)
    far_count = max(1, row_total // 32)
    far_stride = max(1, (row_total // 2 - 1 - reach_near) // far_count)
    distances = [(0, False)]
    for distance in range(1, reach_near + 1):
        distances.append((distance, False))
        distances.append((-distance, False))
    for number in range(far_count):
        distance = row_total // 2 - number * far_stride
        distances.append((distance, True))
        if 2 * distance != row_total:
            distances.append((-distance, True))
    return distances


def split(value):
    high = value.astype(jnp.bfloat16)
    low = (value - high.astype(jnp.float32)).astype(jnp.bfloat16)
    return high, low


def make_kernel(row_total, team_size, slot_count, samples_here, size):
    distances = link_distances(row_total)
    tiles = len(distances)
    used = min(slot_count, tiles)
    groups = team_size // 2
    half_rows = size // 2
    samples = samples_here * team_size

    def kernel(links, counts, w_hbm, x_hbm, out_hbm, y_hbm,
               w_buf, x_buf, y_buf, part, pair_in, half, far_in, full, out_buf,
               local_sem, x_send, x_recv, y_send, y_recv, pair_send, pair_recv,
               far_send, far_recv, full_send, full_recv):
        row = lax.axis_index("blk")
        team = lax.axis_index("team")
        core = lax.rem(team, 2)
        group = team // 2
        other = group * 2 + (1 - core)
        mine = pl.ds(pl.multiple_of(core * half_rows, half_rows), half_rows)
        theirs = pl.ds(pl.multiple_of((1 - core) * half_rows, half_rows), half_rows)

        load_w = pltpu.make_async_copy(w_hbm.at[0, pl.ds(0, used)], w_buf, local_sem.at[0])
        load_w.start()
        load_x = pltpu.make_async_copy(x_hbm.at[0], x_buf.at[0], local_sem.at[1])
        load_x.start()

        def target(t):
            distance, wraps = distances[t]
            there = row - distance
            ok = None if wraps else (there >= 0) & (there < row_total)
            return lax.rem(there + row_total, row_total), ok

        def source_ok(t):
            distance, wraps = distances[t]
            there = row + distance
            return None if wraps else (there >= 0) & (there < row_total)

        def guarded(ok, action):
            if ok is None:
                action()
            else:
                pl.when(ok)(action)

        def far_team(step):
            return lax.rem(group + step, groups) * 2 + core

        barrier = pltpu.get_barrier_semaphore()
        expected = jnp.int32(groups)
        for t in range(1, tiles):
            there, ok = target(t)

            def greet(there=there):
                pl.semaphore_signal(barrier, inc=1, device_id=(there, team), device_id_type=MESH)
            guarded(ok, greet)
            back = source_ok(t)
            expected = expected + (1 if back is None else back.astype(jnp.int32))
        pl.semaphore_signal(barrier, inc=1, device_id=(row, other), device_id_type=MESH)
        for step in range(1, groups):
            pl.semaphore_signal(barrier, inc=1, device_id=(row, far_team(step)), device_id_type=MESH)
        pl.semaphore_wait(barrier, expected)

        def exchange(source, buf, send, recv):
            copies = [None]
            for t in range(1, tiles):
                there, ok = target(t)
                copy = pltpu.make_async_remote_copy(
                    src_ref=source, dst_ref=buf.at[t], send_sem=send.at[t], recv_sem=recv.at[t],
                    device_id=(there, team), device_id_type=MESH)
                guarded(ok, copy.start)
                copies.append(copy)
            return copies

        def arrived(copies, buf, t):
            ok = source_ok(t)
            if ok is None:
                copies[t].wait_recv()
            else:
                pl.when(ok)(copies[t].wait_recv)

                def clear():
                    buf[t] = jnp.zeros_like(buf[t])
                pl.when(jnp.logical_not(ok))(clear)

        def sent(copies):
            for t in range(1, tiles):
                guarded(target(t)[1], copies[t].wait_send)

        x_copies = exchange(x_hbm.at[0], x_buf, x_send, x_recv)

        rest = slot_count - used
        clear_rest = None
        if rest:
            out_buf[pl.ds(used, rest)] = jnp.zeros((rest, size, size), jnp.float32)
            clear_rest = pltpu.make_async_copy(
                out_buf.at[pl.ds(used, rest)], out_hbm.at[0, pl.ds(used, rest)], local_sem.at[3])
            clear_rest.start()

        live_count = counts[0]
        slot_of, is_live = [], []
        for t in range(tiles):
            column = lax.rem(row + distances[t][0] + row_total, row_total)
            slot = jnp.int32(0)
            found = jnp.bool_(False)
            for k in range(used):
                hit = (links[0, k] == column) & (k < live_count)
                slot = jnp.where(hit, k, slot)
                found = found | hit
            slot_of.append(slot)
            is_live.append(found)

        load_w.wait()
        load_x.wait()
        y = None
        for t in range(tiles):
            weight = jnp.where(is_live[t], w_buf[slot_of[t]], 0.0)
            w_high, w_low = split(weight)
            right = jnp.concatenate([w_high, w_low, w_high], axis=1)
            if t:
                arrived(x_copies, x_buf, t)
            high, low = split(x_buf[t])
            left = jnp.concatenate([high, high, low], axis=1)
            term = lax.dot_general(left, right, (((1,), (1,)), ((), ())),
                                   preferred_element_type=jnp.float32)
            y = term if y is None else y + term
        y_buf[0] = y
        y_copies = exchange(y_buf.at[0], y_buf, y_send, y_recv)
        store_y = pltpu.make_async_copy(y_buf.at[0], y_hbm.at[0], local_sem.at[2])
        store_y.start()

        both = jnp.concatenate([y, x_buf[0]], axis=0).T
        high, low = split(both)
        left = jnp.concatenate([high, high, low], axis=1)

        pair_copies, far_copies, full_copies = [], [], []

        def stage_tile(t):
            if t:
                arrived(y_copies, y_buf, t)
            high, low = split(jnp.concatenate([x_buf[t], y_buf[t]], axis=0))
            right = jnp.concatenate([high, low, high], axis=0)
            part[t] = jnp.dot(left, right, preferred_element_type=jnp.float32)
            copy = pltpu.make_async_remote_copy(
                src_ref=part.at[t, theirs], dst_ref=pair_in.at[t],
                send_sem=pair_send.at[t], recv_sem=pair_recv.at[t],
                device_id=(row, other), device_id_type=MESH)
            copy.start()
            pair_copies.append(copy)

        def stage_pair(t):
            pair_copies[t].wait_recv()
            half[t] = part[t, mine] + pair_in[t]
            row_copies = []
            for step in range(1, groups):
                copy = pltpu.make_async_remote_copy(
                    src_ref=half.at[t], dst_ref=far_in.at[step - 1, t],
                    send_sem=far_send.at[step - 1, t], recv_sem=far_recv.at[step - 1, t],
                    device_id=(row, far_team(step)), device_id_type=MESH)
                copy.start()
                row_copies.append(copy)
            far_copies.append(row_copies)

        def stage_far(t):
            total = half[t]
            for step in range(1, groups):
                far_copies[t][step - 1].wait_recv()
                total = total + far_in[step - 1, t]
            full[t, mine] = total
            copy = pltpu.make_async_remote_copy(
                src_ref=full.at[t, mine], dst_ref=full.at[t, mine],
                send_sem=full_send.at[t], recv_sem=full_recv.at[t],
                device_id=(row, other), device_id_type=MESH)
            copy.start()
            full_copies.append(copy)

        stage_tile(0)
        stage_pair(0)
        for t in range(1, tiles):
            stage_tile(t)
        for t in range(1, tiles):
            stage_pair(t)
        for t in range(tiles):
            stage_far(t)
        for t in range(tiles):
            full_copies[t].wait_recv()

        diagonal = (lax.broadcasted_iota(jnp.int32, (size, size), 0)
                    == lax.broadcasted_iota(jnp.int32, (size, size), 1))
        stores = []
        for k in range(used):
            live = k < live_count
            column = links[0, k]
            place = jnp.int32(0)
            for t in range(1, tiles):
                hit = column == lax.rem(row + distances[t][0] + row_total, row_total)
                place = jnp.where(hit, t, place)
            weight = w_buf[k]
            grad = full[place] / (2.0 * samples)
            corner = diagonal & (live & (column == row))
            grad = grad - jnp.where(corner, 1.0 / jnp.where(corner, weight, 1.0), 0.0)
            moved = weight - step_size * grad
            edge = step_size * penalty
            shrunk = moved - jnp.minimum(jnp.maximum(moved, -edge), edge)
            result = jnp.where(corner, moved, shrunk)
            out_buf[k] = jnp.where(live, result, 0.0)
            copy = pltpu.make_async_copy(out_buf.at[k], out_hbm.at[0, k], local_sem.at[4 + k])
            copy.start()
            stores.append(copy)

        sent(x_copies)
        sent(y_copies)
        for t in range(tiles):
            pair_copies[t].wait_send()
            for copy in far_copies[t]:
                copy.wait_send()
            full_copies[t].wait_send()
        store_y.wait()
        if clear_rest is not None:
            clear_rest.wait()
        for copy in stores:
            copy.wait()

    f32 = jnp.float32
    far = max(1, groups - 1)
    dma = pltpu.SemaphoreType.DMA
    scratch = [
        pltpu.VMEM((used, size, size), f32),
        pltpu.VMEM((tiles, samples_here, size), f32),
        pltpu.VMEM((tiles, samples_here, size), f32),
        pltpu.VMEM((tiles, size, size), f32),
        pltpu.VMEM((tiles, half_rows, size), f32),
        pltpu.VMEM((tiles, half_rows, size), f32),
        pltpu.VMEM((far, tiles, half_rows, size), f32),
        pltpu.VMEM((tiles, size, size), f32),
        pltpu.VMEM((slot_count, size, size), f32),
        dma((4 + used,)), dma((tiles,)), dma((tiles,)), dma((tiles,)), dma((tiles,)),
        dma((tiles,)), dma((tiles,)), dma((far, tiles)), dma((far, tiles)),
        dma((tiles,)), dma((tiles,)),
    ]
    return kernel, scratch


def per_device(omega, dosage, columns, counts):
    row_total = lax.axis_size("blk")
    team_size = lax.axis_size("team")
    slot_count, size = omega.shape[1], omega.shape[2]
    samples_here = dosage.shape[1]
    kernel, scratch = make_kernel(row_total, team_size, slot_count, samples_here, size)
    return pl.pallas_call(
        kernel,
        out_shape=(jax.ShapeDtypeStruct(omega.shape, jnp.float32),
                   jax.ShapeDtypeStruct(dosage.shape, jnp.float32)),
        in_specs=[pl.BlockSpec(memory_space=pltpu.SMEM), pl.BlockSpec(memory_space=pltpu.SMEM),
                  pl.BlockSpec(memory_space=pl.ANY), pl.BlockSpec(memory_space=pl.ANY)],
        out_specs=(pl.BlockSpec(memory_space=pl.ANY), pl.BlockSpec(memory_space=pl.ANY)),
        scratch_shapes=scratch,
        compiler_params=pltpu.CompilerParams(
            collective_id=0, has_side_effects=True, vmem_limit_bytes=32 * 1024 * 1024),
    )(columns, counts, omega, dosage)


def solution(mesh):
    return jax.shard_map(
        per_device,
        mesh=mesh,
        in_specs=(P("blk", None, None, None), P("blk", "team", None), P("blk", None), P("blk")),
        out_specs=(P("blk", None, None, None), P("blk", "team", None)),
        check_vma=False,
    )
```

time: 79.4 us -> 25 us (0.31)
  waiting for transfers between devices: 36.4 us -> 0 us
  Pallas kernels: 0 us -> 20 us
  starting transfers between devices: 13.7 us -> 0 us
  between operations: 14.8 us -> 1.32 us
  local copies, waits for them, and re-layouts: 8.85 us -> 3.21 us
  matrix products: 3.68 us -> 0 us
  other arithmetic: 1.65 us -> 0 us
    psum x1 -> x0, waiting for transfers between devices: 34.5 us -> none  [per_device(): summed = lax.psum(tiles, 'team')]
    pallas_call x0 -> x1, Pallas kernels: none -> 20 us  [per_device(): pl.pallas_call(kernel, out_shape=(jax.ShapeDtypeStruct(omega.shape, jnp.f...]
    ppermute x6 -> x0, starting transfers between devices: 13.7 us -> none  [shifted(): return lax.ppermute(block, axis, route)]
    squeeze x1 -> x0, local copies, waits for them, and re-layouts: 5.87 us -> none  [per_device(): weights = omega[0]]
    dot_general x3 -> x0, matrix products: 3.68 us -> none  [the longest x1 1.88 us: per_device(): tiles = jnp.einsum('sa,ksb->kab', product, placed_dosage, precision=highest)]
    unnamed x10 -> x8, local copies, waits for them, and re-layouts: 1.21 us -> 3.21 us
    ppermute x6 -> x0, waiting for transfers between devices: 1.88 us -> none  [shifted(): return lax.ppermute(block, axis, route)]
    gather x1 -> x0, local copies, waits for them, and re-layouts: 1.76 us -> none  [per_device(): jnp.diagonal(weights, axis1=1, axis2=2)]
  transfers between devices with their start and end apart: 7 -> 0, of which waited for: 2 -> 0; matrix products, arithmetic and copies ran while one was open for 10% -> 0% of each run, Pallas kernels for 0% -> 0%
where the time goes in v1:
time: 25 us; the launch traced here: 24.6 us
  Pallas kernels  20 us (80%)
  local copies, waits for them, and re-layouts  3.21 us (13%)
  between operations  1.32 us (5%)
    pallas_call x1, Pallas kernels, per_device(): pl.pallas_call(kernel, out_shape=(jax.ShapeDtypeStruct(omega.shape, jnp.f...  20 us
    unnamed x8, local copies, waits for them, and re-layouts  3.21 us

profile of v1, /device:TPU:0, one launch (start us, length us, event | category | flops | bytes accessed | tf_op | source)
XLA Modules:
  0.0 24.6 jit_solution(11272646647180052650)
XLA Ops:
  0.6 0.0 copy-start.2
  1.3 0.0 copy-done.2
  1.3 0.0 copy-start
  1.3 1.0 %copy-done = f32[1,8,128,128]{3,2,1,0:T(8,128)S(1)} copy-done((f32[1,8,128,128]{3,2,1,0:T(8,128)S(1)}, f32[1,8,128,128]{3,2,1,0:T(8,128)}, u32[]{:S(2)}) %copy-start) | copy-done | bytes 524312
  2.4 0.0 copy-start.1
  2.4 0.8 %copy-done.1 = f32[1,64,128]{2,1,0:T(8,128)S(1)} copy-done((f32[1,64,128]{2,1,0:T(8,128)S(1)}, f32[1,64,128]{2,1,0:T(8,128)}, u32[]{:S(2)}) %copy-start.1) | copy-done | bytes 32792
  3.1 20.0 %shard_map.59 = (f32[1,8,128,128]{3,2,1,0:T(8,128)S(1)}, f32[1,64,128]{2,1,0:T(8,128)S(1)}) custom-call(s32[1,8]{1,0:T(1,128)S(1)} %copy-done.2, s32[1]{0:T(128)S(6)} %copy.8.counts, f32[1,8,128,128]{3,2,1,0:T(8,128)S(1)} %copy-done, f32[1,64,128]{2,1,0:T(8,128)S(1)} %copy-done.1), custom_call_target="tpu_custom_call" | custom-call | tf_op jit(solution)/shard_map/pallas_call | solution.py:281
  23.1 0.8 %copy.9 = f32[1,8,128,128]{3,2,1,0:T(8,128)} copy(f32[1,8,128,128]{3,2,1,0:T(8,128)S(1)} %get-tuple-element.4) | data formatting | bytes 1048576
  23.9 0.6 %copy.10 = f32[1,64,128]{2,1,0:T(8,128)} copy(f32[1,64,128]{2,1,0:T(8,128)S(1)} %get-tuple-element.5) | data formatting | bytes 65536
Async XLA Ops:
  0.6 0.7 %copy-start.2 = (s32[1,8]{1,0:T(1,128)S(1)}, s32[1,8]{1,0:T(1,128)}, u32[]{:S(2)}) copy-start(s32[1,8]{1,0:T(1,128)} %links.1) | copy-start | bytes 100
  1.3 1.0 %copy-start = (f32[1,8,128,128]{3,2,1,0:T(8,128)S(1)}, f32[1,8,128,128]{3,2,1,0:T(8,128)}, u32[]{:S(2)}) copy-start(f32[1,8,128,128]{3,2,1,0:T(8,128)} %w_hbm.1) | copy-start | bytes 1572868
  2.4 0.8 %copy-start.1 = (f32[1,64,128]{2,1,0:T(8,128)S(1)}, f32[1,64,128]{2,1,0:T(8,128)}, u32[]{:S(2)}) copy-start(f32[1,64,128]{2,1,0:T(8,128)} %x_hbm.1) | copy-start | bytes 98308

commit v2 on v1

--- a/solution.py
+++ b/solution.py
@@ -40,8 +40,8 @@
     half_rows = size // 2
     samples = samples_here * team_size
 
-    def kernel(links, counts, w_hbm, x_hbm, out_hbm, y_hbm,
-               w_buf, x_buf, y_buf, part, pair_in, half, far_in, full, out_buf,
+    def kernel(links_hbm, w_hbm, x_hbm, out_buf, y_out,
+               links, w_buf, x_buf, y_buf, part, pair_in, half, far_in, full,
                local_sem, x_send, x_recv, y_send, y_recv, pair_send, pair_recv,
                far_send, far_recv, full_send, full_recv):
         row = lax.axis_index("blk")
@@ -56,6 +56,8 @@
         load_w.start()
         load_x = pltpu.make_async_copy(x_hbm.at[0], x_buf.at[0], local_sem.at[1])
         load_x.start()
+        load_links = pltpu.make_async_copy(links_hbm, links, local_sem.at[2])
+        load_links.start()
 
         def target(t):
             distance, wraps = distances[t]
@@ -121,21 +123,18 @@
         x_copies = exchange(x_hbm.at[0], x_buf, x_send, x_recv)
 
         rest = slot_count - used
-        clear_rest = None
         if rest:
-            out_buf[pl.ds(used, rest)] = jnp.zeros((rest, size, size), jnp.float32)
-            clear_rest = pltpu.make_async_copy(
-                out_buf.at[pl.ds(used, rest)], out_hbm.at[0, pl.ds(used, rest)], local_sem.at[3])
-            clear_rest.start()
-
-        live_count = counts[0]
+            out_buf[0, pl.ds(used, rest)] = jnp.zeros((rest, size, size), jnp.float32)
+
+        load_links.wait()
+        live_slot = [jnp.bool_(True)] + [links[0, k] > links[0, k - 1] for k in range(1, used)]
         slot_of, is_live = [], []
         for t in range(tiles):
             column = lax.rem(row + distances[t][0] + row_total, row_total)
             slot = jnp.int32(0)
             found = jnp.bool_(False)
             for k in range(used):
-                hit = (links[0, k] == column) & (k < live_count)
+                hit = (links[0, k] == column) & live_slot[k]
                 slot = jnp.where(hit, k, slot)
                 found = found | hit
             slot_of.append(slot)
@@ -157,8 +156,7 @@
             y = term if y is None else y + term
         y_buf[0] = y
         y_copies = exchange(y_buf.at[0], y_buf, y_send, y_recv)
-        store_y = pltpu.make_async_copy(y_buf.at[0], y_hbm.at[0], local_sem.at[2])
-        store_y.start()
+        y_out[0] = y
 
         both = jnp.concatenate([y, x_buf[0]], axis=0).T
         high, low = split(both)
@@ -218,9 +216,8 @@
 
         diagonal = (lax.broadcasted_iota(jnp.int32, (size, size), 0)
                     == lax.broadcasted_iota(jnp.int32, (size, size), 1))
-        stores = []
         for k in range(used):
-            live = k < live_count
+            live = live_slot[k]
             column = links[0, k]
             place = jnp.int32(0)
             for t in range(1, tiles):
@@ -234,10 +231,7 @@
             edge = step_size * penalty
             shrunk = moved - jnp.minimum(jnp.maximum(moved, -edge), edge)
             result = jnp.where(corner, moved, shrunk)
-            out_buf[k] = jnp.where(live, result, 0.0)
-            copy = pltpu.make_async_copy(out_buf.at[k], out_hbm.at[0, k], local_sem.at[4 + k])
-            copy.start()
-            stores.append(copy)
+            out_buf[0, k] = jnp.where(live, result, 0.0)
 
         sent(x_copies)
         sent(y_copies)
@@ -246,16 +240,12 @@
             for copy in far_copies[t]:
                 copy.wait_send()
             full_copies[t].wait_send()
-        store_y.wait()
-        if clear_rest is not None:
-            clear_rest.wait()
-        for copy in stores:
-            copy.wait()
 
     f32 = jnp.float32
     far = max(1, groups - 1)
     dma = pltpu.SemaphoreType.DMA
     scratch = [
+        pltpu.SMEM((1, slot_count), jnp.int32),
         pltpu.VMEM((used, size, size), f32),
         pltpu.VMEM((tiles, samples_here, size), f32),
         pltpu.VMEM((tiles, samples_here, size), f32),
@@ -264,12 +254,20 @@
         pltpu.VMEM((tiles, half_rows, size), f32),
         pltpu.VMEM((far, tiles, half_rows, size), f32),
         pltpu.VMEM((tiles, size, size), f32),
-        pltpu.VMEM((slot_count, size, size), f32),
-        dma((4 + used,)), dma((tiles,)), dma((tiles,)), dma((tiles,)), dma((tiles,)),
+        dma((3,)), dma((tiles,)), dma((tiles,)), dma((tiles,)), dma((tiles,)),
         dma((tiles,)), dma((tiles,)), dma((far, tiles)), dma((far, tiles)),
         dma((tiles,)), dma((tiles,)),
     ]
     return kernel, scratch
+
+
+def write_out(omega_in, y_in, omega_out, y_out, sem):
+    first = pltpu.make_async_copy(omega_in, omega_out, sem.at[0])
+    second = pltpu.make_async_copy(y_in, y_out, sem.at[1])
+    first.start()
+    second.start()
+    first.wait()
+    second.wait()
 
 
 def per_device(omega, dosage, columns, counts):
@@ -278,17 +276,25 @@
     slot_count, size = omega.shape[1], omega.shape[2]
     samples_here = dosage.shape[1]
     kernel, scratch = make_kernel(row_total, team_size, slot_count, samples_here, size)
-    return pl.pallas_call(
+    shapes = (jax.ShapeDtypeStruct(omega.shape, jnp.float32),
+              jax.ShapeDtypeStruct(dosage.shape, jnp.float32))
+    results = pl.pallas_call(
         kernel,
-        out_shape=(jax.ShapeDtypeStruct(omega.shape, jnp.float32),
-                   jax.ShapeDtypeStruct(dosage.shape, jnp.float32)),
-        in_specs=[pl.BlockSpec(memory_space=pltpu.SMEM), pl.BlockSpec(memory_space=pltpu.SMEM),
-                  pl.BlockSpec(memory_space=pl.ANY), pl.BlockSpec(memory_space=pl.ANY)],
-        out_specs=(pl.BlockSpec(memory_space=pl.ANY), pl.BlockSpec(memory_space=pl.ANY)),
+        out_shape=shapes,
+        in_specs=[pl.BlockSpec(memory_space=pltpu.HBM)] * 3,
+        out_specs=(pl.BlockSpec(memory_space=pltpu.VMEM), pl.BlockSpec(memory_space=pltpu.VMEM)),
         scratch_shapes=scratch,
         compiler_params=pltpu.CompilerParams(
-            collective_id=0, has_side_effects=True, vmem_limit_bytes=32 * 1024 * 1024),
-    )(columns, counts, omega, dosage)
+            collective_id=0, has_side_effects=True, vmem_limit_bytes=24 * 1024 * 1024),
+    )(*[pltpu.with_memory_space_constraint(value, pltpu.HBM)
+        for value in (columns, omega, dosage)])
+    return pl.pallas_call(
+        write_out,
+        out_shape=shapes,
+        in_specs=[pl.BlockSpec(memory_space=pl.ANY)] * 2,
+        out_specs=(pl.BlockSpec(memory_space=pltpu.HBM), pl.BlockSpec(memory_space=pltpu.HBM)),
+        scratch_shapes=[pltpu.SemaphoreType.DMA((2,))],
+    )(*[pltpu.with_memory_space_constraint(value, pltpu.VMEM) for value in results])
 
 
 def solution(mesh):

time: 25 us -> 21 us (0.84)
  local copies, waits for them, and re-layouts: 3.21 us -> 0 us
  between operations: 1.32 us -> 0.64 us
    unnamed x8 -> x0, local copies, waits for them, and re-layouts: 3.21 us -> none
    pallas_call x1 -> x2, Pallas kernels: 20 us -> 20.2 us  [the longest x1 19.3 us: per_device(): pl.pallas_call(kernel, out_shape=shapes, in_specs=[pl.BlockSpec(memory_sp...]
where the time goes in v2:
time: 21 us; the launch traced here: 20.8 us
  Pallas kernels  20.2 us (96%)
  between operations  0.64 us (3%)
    pallas_call x1, Pallas kernels, per_device(): pl.pallas_call(kernel, out_shape=shapes, in_specs=[pl.BlockSpec(memory_sp...  19.3 us
    pallas_call x1, Pallas kernels, per_device(): pl.pallas_call(write_out, out_shape=shapes, in_specs=[pl.BlockSpec(memory...  0.81 us

profile of v2, /device:TPU:0, one launch (start us, length us, event | category | flops | bytes accessed | tf_op | source)
XLA Modules:
  0.0 20.8 jit_solution(5355277373984325498)
XLA Ops:
  0.6 19.3 %shard_map.50 = (f32[1,8,128,128]{3,2,1,0:T(8,128)S(1)}, f32[1,64,128]{2,1,0:T(8,128)S(1)}) custom-call(s32[1,8]{1,0:T(1,128)} %links_hbm.1, f32[1,8,128,128]{3,2,1,0:T(8,128)} %w_hbm.1, f32[1,64,128]{2,1,0:T(8,128)} %x_hbm.1), custom_call_target="tpu_custom_call" | custom-call | tf_op jit(solution)/shard_map/pallas_call | solution.py:281
  20.0 0.8 %shard_map.51 = (f32[1,8,128,128]{3,2,1,0:T(8,128)}, f32[1,64,128]{2,1,0:T(8,128)}) custom-call(f32[1,8,128,128]{3,2,1,0:T(8,128)S(1)} %get-tuple-element.4.omega_in, f32[1,64,128]{2,1,0:T(8,128)S(1)} %get-tuple-element.5.y_in), custom_call_target="tpu_custom_call" | custom-call | tf_op jit(solution)/shard_map/pallas_call | solution.py:291

commit v3 on v2

--- a/solution.py
+++ b/solution.py
@@ -35,15 +35,19 @@
 def make_kernel(row_total, team_size, slot_count, samples_here, size):
     distances = link_distances(row_total)
     tiles = len(distances)
+    steps = [distance for distance, _ in distances]
+    opposite = [t if 2 * abs(step) == row_total else steps.index(-step)
+                for t, step in enumerate(steps)]
     used = min(slot_count, tiles)
     groups = team_size // 2
     half_rows = size // 2
     samples = samples_here * team_size
 
     def kernel(links_hbm, w_hbm, x_hbm, out_buf, y_out,
-               links, w_buf, x_buf, y_buf, part, pair_in, half, far_in, full,
-               local_sem, x_send, x_recv, y_send, y_recv, pair_send, pair_recv,
-               far_send, far_recv, full_send, full_recv):
+               links, w_buf, x_buf, part, pair_in, half, far_in, back_in, full, back,
+               local_sem, x_send, x_recv, pair_send, pair_recv,
+               far_send, far_recv, full_send, full_recv,
+               row_send, row_recv, back_send, back_recv):
         row = lax.axis_index("blk")
         team = lax.axis_index("team")
         core = lax.rem(team, 2)
@@ -85,24 +89,26 @@
             there, ok = target(t)
 
             def greet(there=there):
-                pl.semaphore_signal(barrier, inc=1, device_id=(there, team), device_id_type=MESH)
+                for step in range(groups):
+                    pl.semaphore_signal(barrier, inc=1, device_id=(there, far_team(step)),
+                                        device_id_type=MESH)
             guarded(ok, greet)
-            back = source_ok(t)
-            expected = expected + (1 if back is None else back.astype(jnp.int32))
+            ok = source_ok(t)
+            expected = expected + (groups if ok is None else groups * ok.astype(jnp.int32))
         pl.semaphore_signal(barrier, inc=1, device_id=(row, other), device_id_type=MESH)
         for step in range(1, groups):
             pl.semaphore_signal(barrier, inc=1, device_id=(row, far_team(step)), device_id_type=MESH)
         pl.semaphore_wait(barrier, expected)
 
         def exchange(source, buf, send, recv):
-            copies = [None]
-            for t in range(1, tiles):
+            copies = {}
+            for t in reversed(range(1, tiles)):
                 there, ok = target(t)
                 copy = pltpu.make_async_remote_copy(
                     src_ref=source, dst_ref=buf.at[t], send_sem=send.at[t], recv_sem=recv.at[t],
                     device_id=(there, team), device_id_type=MESH)
                 guarded(ok, copy.start)
-                copies.append(copy)
+                copies[t] = copy
             return copies
 
         def arrived(copies, buf, t):
@@ -120,7 +126,8 @@
             for t in range(1, tiles):
                 guarded(target(t)[1], copies[t].wait_send)
 
-        x_copies = exchange(x_hbm.at[0], x_buf, x_send, x_recv)
+        load_x.wait()
+        x_copies = exchange(x_buf.at[0], x_buf, x_send, x_recv)
 
         rest = slot_count - used
         if rest:
@@ -141,7 +148,6 @@
             is_live.append(found)
 
         load_w.wait()
-        load_x.wait()
         y = None
         for t in range(tiles):
             weight = jnp.where(is_live[t], w_buf[slot_of[t]], 0.0)
@@ -154,41 +160,48 @@
             term = lax.dot_general(left, right, (((1,), (1,)), ((), ())),
                                    preferred_element_type=jnp.float32)
             y = term if y is None else y + term
-        y_buf[0] = y
-        y_copies = exchange(y_buf.at[0], y_buf, y_send, y_recv)
         y_out[0] = y
 
-        both = jnp.concatenate([y, x_buf[0]], axis=0).T
-        high, low = split(both)
-        left = jnp.concatenate([high, high, low], axis=1)
-
-        pair_copies, far_copies, full_copies = [], [], []
+        high, low = split(y)
+        left = jnp.concatenate([high, high, low, low], axis=0).astype(jnp.float32).T
+        left = left.astype(jnp.bfloat16)
+
+        pair_copies, far_copies, full_copies, row_copies, back_copies = {}, {}, {}, {}, {}
 
         def stage_tile(t):
-            if t:
-                arrived(y_copies, y_buf, t)
-            high, low = split(jnp.concatenate([x_buf[t], y_buf[t]], axis=0))
-            right = jnp.concatenate([high, low, high], axis=0)
+            high, low = split(x_buf[t])
+            right = jnp.concatenate([high, low, high, low], axis=0)
             part[t] = jnp.dot(left, right, preferred_element_type=jnp.float32)
-            copy = pltpu.make_async_remote_copy(
+            pair_copies[t] = pltpu.make_async_remote_copy(
                 src_ref=part.at[t, theirs], dst_ref=pair_in.at[t],
                 send_sem=pair_send.at[t], recv_sem=pair_recv.at[t],
                 device_id=(row, other), device_id_type=MESH)
-            copy.start()
-            pair_copies.append(copy)
+            pair_copies[t].start()
 
         def stage_pair(t):
             pair_copies[t].wait_recv()
             half[t] = part[t, mine] + pair_in[t]
-            row_copies = []
+            if t:
+                u = opposite[t]
+                there, ok = target(u)
+                row_copies[u] = [pltpu.make_async_remote_copy(
+                    src_ref=half.at[t], dst_ref=back_in.at[step, u],
+                    send_sem=row_send.at[step, u], recv_sem=row_recv.at[step, u],
+                    device_id=(there, far_team(step)), device_id_type=MESH)
+                    for step in range(groups)]
+
+                def send_rows():
+                    for copy in reversed(row_copies[u]):
+                        copy.start()
+                guarded(ok, send_rows)
+            far_copies[t] = []
             for step in range(1, groups):
                 copy = pltpu.make_async_remote_copy(
                     src_ref=half.at[t], dst_ref=far_in.at[step - 1, t],
                     send_sem=far_send.at[step - 1, t], recv_sem=far_recv.at[step - 1, t],
                     device_id=(row, far_team(step)), device_id_type=MESH)
                 copy.start()
-                row_copies.append(copy)
-            far_copies.append(row_copies)
+                far_copies[t].append(copy)
 
         def stage_far(t):
             total = half[t]
@@ -196,23 +209,43 @@
                 far_copies[t][step - 1].wait_recv()
                 total = total + far_in[step - 1, t]
             full[t, mine] = total
-            copy = pltpu.make_async_remote_copy(
+            full_copies[t] = pltpu.make_async_remote_copy(
                 src_ref=full.at[t, mine], dst_ref=full.at[t, mine],
                 send_sem=full_send.at[t], recv_sem=full_recv.at[t],
                 device_id=(row, other), device_id_type=MESH)
-            copy.start()
-            full_copies.append(copy)
-
-        stage_tile(0)
-        stage_pair(0)
-        for t in range(1, tiles):
+            full_copies[t].start()
+
+        def stage_back(u):
+            back_copies[u] = pltpu.make_async_remote_copy(
+                src_ref=back.at[u, mine], dst_ref=back.at[u, mine],
+                send_sem=back_send.at[u], recv_sem=back_recv.at[u],
+                device_id=(row, other), device_id_type=MESH)
+
+            def forward():
+                for copy in row_copies[u]:
+                    copy.wait_recv()
+                total = back_in[0, u]
+                for step in range(1, groups):
+                    total = total + back_in[step, u]
+                back[u, mine] = total
+                back_copies[u].start()
+            guarded(source_ok(u), forward)
+
+        order = list(reversed(range(tiles)))
+        for i, t in enumerate(order):
             stage_tile(t)
-        for t in range(1, tiles):
-            stage_pair(t)
-        for t in range(tiles):
+            if i:
+                stage_pair(order[i - 1])
+        stage_pair(order[-1])
+        for t in order:
             stage_far(t)
-        for t in range(tiles):
+        for t in order[:-1]:
+            stage_back(opposite[t])
+        for t in order:
             full_copies[t].wait_recv()
+        back[0] = full[0]
+        for t in order[:-1]:
+            guarded(source_ok(t), back_copies[t].wait_recv)
 
         diagonal = (lax.broadcasted_iota(jnp.int32, (size, size), 0)
                     == lax.broadcasted_iota(jnp.int32, (size, size), 1))
@@ -224,7 +257,7 @@
                 hit = column == lax.rem(row + distances[t][0] + row_total, row_total)
                 place = jnp.where(hit, t, place)
             weight = w_buf[k]
-            grad = full[place] / (2.0 * samples)
+            grad = (full[place] + back[place].T) / (2.0 * samples)
             corner = diagonal & (live & (column == row))
             grad = grad - jnp.where(corner, 1.0 / jnp.where(corner, weight, 1.0), 0.0)
             moved = weight - step_size * grad
@@ -234,7 +267,11 @@
             out_buf[0, k] = jnp.where(live, result, 0.0)
 
         sent(x_copies)
-        sent(y_copies)
+        for t in range(1, tiles):
+            for copy in row_copies[t]:
+                guarded(target(t)[1], copy.wait_send)
+        for t in range(1, tiles):
+            guarded(source_ok(t), back_copies[t].wait_send)
         for t in range(tiles):
             pair_copies[t].wait_send()
             for copy in far_copies[t]:
@@ -248,14 +285,16 @@
         pltpu.SMEM((1, slot_count), jnp.int32),
         pltpu.VMEM((used, size, size), f32),
         pltpu.VMEM((tiles, samples_here, size), f32),
-        pltpu.VMEM((tiles, samples_here, size), f32),
         pltpu.VMEM((tiles, size, size), f32),
         pltpu.VMEM((tiles, half_rows, size), f32),
         pltpu.VMEM((tiles, half_rows, size), f32),
         pltpu.VMEM((far, tiles, half_rows, size), f32),
+        pltpu.VMEM((groups, tiles, half_rows, size), f32),
         pltpu.VMEM((tiles, size, size), f32),
-        dma((3,)), dma((tiles,)), dma((tiles,)), dma((tiles,)), dma((tiles,)),
+        pltpu.VMEM((tiles, size, size), f32),
+        dma((3,)), dma((tiles,)), dma((tiles,)),
         dma((tiles,)), dma((tiles,)), dma((far, tiles)), dma((far, tiles)),
+        dma((tiles,)), dma((tiles,)), dma((groups, tiles)), dma((groups, tiles)),
         dma((tiles,)), dma((tiles,)),
     ]
     return kernel, scratch

time: 21 us -> 19.6 us (0.933)
  Pallas kernels: 20.2 us -> 18.8 us
    pallas_call x1, Pallas kernels: 19.3 us -> 18 us  [per_device(): pl.pallas_call(kernel, out_shape=shapes, in_specs=[pl.BlockSpec(memory_sp...]
where the time goes in v3:
time: 19.6 us; the launch traced here: 19.4 us
  Pallas kernels  18.8 us (96%)
  between operations  0.64 us (3%)
    pallas_call x1, Pallas kernels, per_device(): pl.pallas_call(kernel, out_shape=shapes, in_specs=[pl.BlockSpec(memory_sp...  18 us
    pallas_call x1, Pallas kernels, per_device(): pl.pallas_call(write_out, out_shape=shapes, in_specs=[pl.BlockSpec(memory...  0.81 us

profile of v3, /device:TPU:0, one launch (start us, length us, event | category | flops | bytes accessed | tf_op | source)
XLA Modules:
  0.0 19.4 jit_solution(12842687236427397959)
XLA Ops:
  0.6 18.0 %shard_map.50 = (f32[1,8,128,128]{3,2,1,0:T(8,128)S(1)}, f32[1,64,128]{2,1,0:T(8,128)S(1)}) custom-call(s32[1,8]{1,0:T(1,128)} %links_hbm.1, f32[1,8,128,128]{3,2,1,0:T(8,128)} %w_hbm.1, f32[1,64,128]{2,1,0:T(8,128)} %x_hbm.1), custom_call_target="tpu_custom_call" | custom-call | tf_op jit(solution)/shard_map/pallas_call | solution.py:320
  18.6 0.8 %shard_map.51 = (f32[1,8,128,128]{3,2,1,0:T(8,128)}, f32[1,64,128]{2,1,0:T(8,128)}) custom-call(f32[1,8,128,128]{3,2,1,0:T(8,128)S(1)} %get-tuple-element.4.omega_in, f32[1,64,128]{2,1,0:T(8,128)S(1)} %get-tuple-element.5.y_in), custom_call_target="tpu_custom_call" | custom-call | tf_op jit(solution)/shard_map/pallas_call | solution.py:330
